TPU v7x, 32 devices: a whole 2x2x4 slice. The times are simulated.
32 devices in a mesh: seq: 16 (over z, y, core), tp: 2 (over x).
Axes of the slice: x: 2, y: 2, z: 4, core: 2. Of those that a mesh axis runs over, the one named last changes fastest.
Arguments:
- qkv_se: bfloat16 [8192, 3, 4096], P('seq', None, 'tp'), may hold values from -6 to 6
- residual: bfloat16 [8192, 4096], P('seq', 'tp'), may hold values from -108 to 108
- taps_se: bfloat16 [256, 7], P('tp'), may hold values from -2 to 2
- skip_se: bfloat16 [4096], P('tp'), may hold values from 0.5 to 1.5
- w_out: bfloat16 [4096, 4096], P('tp', 'seq'), may hold values from -0.125 to 0.125
- norm_gain: bfloat16 [4096], replicated, may hold values from 0.5 to 1.5
- w_in: bfloat16 [4096, 3, 4096], P('seq', None, 'tp'), may hold values from -0.09375 to 0.09375
- taps_mr: bfloat16 [256, 128], P('tp'), may hold values from -0.5 to 0.5
- skip_mr: bfloat16 [4096], P('tp'), may hold values from 0.5 to 1.5
Outputs:
- mixed: bfloat16 [8192, 4096], P('seq', 'tp')
All inputs are finite; a program needn't handle non-finite values.
Results may differ from a plain program's by a relative error of at most 0.0085.
Values may be sent and summed in bfloat16 or wider, within the bound.
A program may use at most 128 MiB of HBM per device.

v0:
```python
import jax
import jax.numpy as jnp
from jax import lax
from jax.sharding import PartitionSpec as P

GROUP = 16
SE_TAPS = 7
MR_TAPS = 128


norm_eps = 1e-05


def shifted(block, axis, distance):
    devices = range(lax.axis_size(axis))
    route = [(i - distance, i) for i in devices if i - distance in devices]
    return lax.ppermute(block, axis, route)


def toeplitz_pair(taps):
    offsets = lax.broadcasted_iota(jnp.int32, (MR_TAPS, MR_TAPS), 0) - lax.broadcasted_iota(
        jnp.int32, (MR_TAPS, MR_TAPS), 1
    )
    lag_ids = lax.broadcasted_iota(jnp.int32, (MR_TAPS, MR_TAPS, MR_TAPS), 0)
    picks = (jnp.remainder(offsets, MR_TAPS)[None] == lag_ids).astype(jnp.bfloat16)
    table = jnp.einsum("gj,jts->gts", taps, picks, preferred_element_type=jnp.float32).astype(
        jnp.bfloat16
    )
    lower = jnp.where(offsets[None] >= 0, table, jnp.zeros_like(table))
    upper = jnp.where(offsets[None] < 0, table, jnp.zeros_like(table))
    return (lower, upper)


def project_out(y_se, w_out):
    return jnp.dot(
        y_se, lax.all_gather(w_out, "seq", axis=1, tiled=True), preferred_element_type=jnp.float32
    )


def per_device(qkv_se, residual, taps_se, skip_se, w_out, norm_gain, w_in, taps_mr, skip_mr):
    row_count = qkv_se.shape[0]
    chan_width = qkv_se.shape[2]
    local_groups = chan_width // GROUP
    query_se = qkv_se[:, 0].astype(jnp.float32)
    u_se = (qkv_se[:, 1].astype(jnp.float32) * qkv_se[:, 2].astype(jnp.float32)).astype(
        jnp.bfloat16
    )
    incoming_se = shifted(u_se[row_count - (SE_TAPS - 1) :], "seq", 1)
    extended = jnp.concatenate([incoming_se, u_se], axis=0).astype(jnp.float32)
    per_channel = jnp.repeat(taps_se.astype(jnp.float32), GROUP, axis=0)
    conv_se = jnp.zeros((row_count, chan_width), jnp.float32)
    for tap_index in range(SE_TAPS):
        begin = SE_TAPS - 1 - tap_index
        conv_se = conv_se + per_channel[:, tap_index] * extended[begin : begin + row_count]
    y_se = (query_se * (conv_se + skip_se.astype(jnp.float32) * u_se.astype(jnp.float32))).astype(
        jnp.bfloat16
    )
    gain_full = norm_gain.astype(jnp.float32)
    partial_out = project_out(y_se, w_out)
    share = lax.psum_scatter(partial_out, "tp", scatter_dimension=1, tiled=True)
    stream = residual.astype(jnp.float32) + share
    squares = lax.psum(jnp.sum(stream * stream, axis=1), "tp")
    scale = lax.rsqrt(squares / (chan_width * lax.axis_size("tp")) + norm_eps)
    my_gain = lax.dynamic_slice_in_dim(gain_full, lax.axis_index("tp") * chan_width, chan_width, 0)
    normed = (stream * scale[:, None] * my_gain).astype(jnp.bfloat16)
    gathered = lax.all_gather(normed, "tp", axis=1, tiled=True)
    piece = lax.all_gather(w_in, "seq", axis=0, tiled=True)
    flat_piece = piece.reshape(piece.shape[0], 3 * chan_width)
    proj = jnp.dot(gathered, flat_piece, preferred_element_type=jnp.float32).reshape(
        row_count, 3, chan_width
    )
    query_mr = proj[:, 0]
    u_mr = (proj[:, 1] * proj[:, 2]).astype(jnp.bfloat16)
    lower, upper = toeplitz_pair(taps_mr)
    block_count = row_count // MR_TAPS
    blocks = u_mr.reshape(block_count, MR_TAPS, local_groups, GROUP)
    inside = jnp.einsum("gts,bsgc->btgc", lower, blocks, preferred_element_type=jnp.float32)
    tail_rows = shifted(blocks[block_count - 1], "seq", 1)
    earlier = jnp.concatenate([tail_rows[None], blocks[: block_count - 1]], axis=0)
    conv_mr = inside + jnp.einsum(
        "gts,bsgc->btgc", upper, earlier, preferred_element_type=jnp.float32
    )
    conv_mr = conv_mr.reshape(row_count, chan_width)
    return (query_mr * (conv_mr + skip_mr.astype(jnp.float32) * u_mr.astype(jnp.float32))).astype(
        jnp.bfloat16
    )


def solution(mesh):
    placed = (
        P("seq", None, "tp"),
        P("seq", "tp"),
        P("tp", None),
        P("tp"),
        P("tp", "seq"),
        P(),
        P("seq", None, "tp"),
        P("tp", None),
        P("tp"),
    )
    return jax.shard_map(
        per_device, mesh=mesh, in_specs=placed, out_specs=P("seq", "tp"), check_vma=False
    )
```

profile of v0, /device:TPU:1, one launch (start us, length us, event | category | flops | bytes accessed | tf_op | source)
XLA Modules:
  0.0 709.7 jit_solution(4292735505262331038)
XLA Ops:
  7.3 3.0 multiply_convert_fusion.1
  10.4 4.5 collective-permute-start
  15.3 3.0 fusion.51
  21.1 121.3 %all-gather.4.cloned.1.call-done = bf16[2048,4096]{1,0:T(8,128)(2,1)} async-done(((bf16[2048,256]{1,0:T(8,128)(2,1)}), bf16[2048,4096]{1,0:T(8,128)(2,1)}) %all-gather.4.cloned.1.call-update) | async-done | bytes 16777232 | tf_op jit(solution)/shard_map/all_gather | solution.py:36
  142.4 27.0 %fusion.19 = f32[512,4096]{1,0:T(8,128)} fusion(bf16[2048,4096]{1,0:T(8,128)(2,1)} %all-gather.4.cloned.1.call-done, f32[518,2048]{1,0:T(8,128)} %maximum_convert_fusion, f32[2048]{0:T(1024)S(1)} %convert_element_type.78, f32[2048]{0:T(1024)S(1)} %bitcast.80, f32[2048]{0:T(1024)S(1)} %bitcast.81, f32[2048]{0:T(1024)S(1)} %bitcast.82, ...), kind=kOutput, calls=%fused_computation.39 | convolution fusion | flops 8609857536 | bytes 58785792 | tf_op jit(solution)/shard_map/dot_general | solution.py:35
  170.1 96.5 %reduce-scatter.2.cloned.1.call-done = f32[512,2048]{1,0:T(8,128)} async-done(((f32[512,4096]{1,0:T(8,128)}), f32[512,2048]{1,0:T(8,128)}) %reduce-scatter.2.cloned.1.call-update) | async-done | bytes 4194320 | tf_op jit(solution)/shard_map/reduce_scatter | solution.py:60
  266.6 2.8 multiply_reduce_fusion
  269.4 3.8 psum.7
  273.2 4.1 multiply_convert_fusion
  277.6 4.7 copy.27
  282.4 53.0 %all-gather.6.cloned.1.call-done = bf16[512,4096]{1,0:T(8,128)(2,1)} async-done(((bf16[512,2048]{1,0:T(8,128)(2,1)}), bf16[512,4096]{1,0:T(8,128)(2,1)}) %all-gather.6.cloned.1.call-update) | async-done | bytes 4194320 | tf_op jit(solution)/shard_map/all_gather | solution.py:66
  335.4 259.0 %all-gather.8.cloned.1.call-done = bf16[4096,3,2048]{0,2,1:T(8,128)(2,1)} async-done(((bf16[256,3,2048]{0,2,1:T(8,128)(2,1)}), bf16[4096,3,2048]{0,2,1:T(8,128)(2,1)}) %all-gather.8.cloned.1.call-update) | async-done | bytes 50331664 | tf_op jit(solution)/shard_map/all_gather | solution.py:67
  594.4 34.3 %fusion = f32[512,3,2048]{2,0,1:T(8,128)} fusion(bf16[4096,3,2048]{0,2,1:T(8,128)(2,1)} %all-gather.8.cloned.1.call-done, bf16[512,4096]{1,0:T(8,128)(2,1)} %all-gather.6.cloned.1.call-done), kind=kOutput, calls=%fused_computation | convolution fusion | flops 25769803776 | bytes 67108864 | tf_op jit(solution)/shard_map/dot_general | solution.py:69
  628.7 4.1 fusion.3
  633.2 3.5 collective-permute-start.1
  636.7 10.4 %select_bitcast_fusion = (bf16[128,128,128,1]{0,2,1,3:T(8,128)(2,1)}, bf16[128,128,128,1]{0,2,1,3:T(8,128)(2,1)}) fusion(pred[128,128]{1,0:T(8,128)(4,1)S(1)} %get-tuple-element.14, pred[128,128]{1,0:T(8,128)(4,1)S(1)} %get-tuple-element.15, bf16[128,128]{1,0:T(8,128)(2,1)S(1)} %copy-done, s32[128,128]{1,0:T(8,128)S(1)} %add_select_fusion), kind=kOutput, calls=%fused_computation.30 | convolution fusion | flops 545259520 | bytes 8519680 | tf_op jit(solution)/shard_map/gj,jts->gts/dot_general | solution.py:26
  647.0 6.7 copy.37
  653.7 6.8 copy.38
  663.0 4.1 convert_element_type.84
  668.7 5.3 slice.102
  675.9 5.3 fusion.25
  681.2 3.0 add_bitcast_fusion
  688.7 5.4 copy.36
  694.0 9.1 %fusion.5 = bf16[512,2048]{1,0:T(8,128)(2,1)} fusion(f32[512,3,2048]{2,0,1:T(8,128)} %fusion, f32[512,2048]{1,0:T(8,128)} %copy.36, f32[2048]{0:T(1024)S(1)} %convert_element_type.86), kind=kLoop, calls=%fused_computation.9 | loop fusion | flops 7340032 | bytes 18882560 | tf_op jit(solution)/shard_map/convert_element_type | solution.py:84
  (48 shorter events, 15.6 us)
Async XLA Ops:
  6.5 630.1 %copy-start = (bf16[128,128]{1,0:T(8,128)(2,1)S(1)}, bf16[128,128]{1,0:T(8,128)(2,1)}, u32[]{:S(2)}) copy-start(bf16[128,128]{1,0:T(8,128)(2,1)} %param.16) | copy-start | bytes 98308
  6.5 8.4 %copy-start.7 = (bf16[128,7]{0,1:T(8,128)(2,1)S(1)}, bf16[128,7]{0,1:T(8,128)(2,1)}, u32[]{:S(2)}) copy-start(bf16[128,7]{0,1:T(8,128)(2,1)} %param.11) | copy-start | bytes 5380
  6.5 135.9 %all-gather.4.cloned.1.call-start = ((), (), s32[]{:S(2)}) async-start(), calls=%async_computation.1 | async-start | bytes 17825792 | tf_op jit(solution)/shard_map/all_gather | solution.py:36
  7.3 259.3 %reduce-scatter.2.cloned.1.call-start = ((), (), s32[]{:S(2)}) async-start(), calls=%async_computation.2 | async-start | bytes 12582912 | tf_op jit(solution)/shard_map/reduce_scatter | solution.py:60
  10.3 8.1 %copy-start.5 = (bf16[2048]{0:T(1024)(128)(2,1)S(1)}, bf16[2048]{0:T(1024)(128)(2,1)}, u32[]{:S(2)}) copy-start(bf16[2048]{0:T(1024)(128)(2,1)} %param.12) | copy-start | bytes 12292
  10.4 8.1 %collective-permute-start = (bf16[6,2048]{1,0:T(8,128)(2,1)S(1)}, bf16[6,2048]{1,0:T(8,128)(2,1)S(1)}, u32[]{:S(2)}, u32[]{:S(2)}) collective-permute-start(bf16[6,2048]{1,0:T(8,128)(2,1)S(1)} %slice_bitcast_fusion.1), channel_id=1, source_target_pairs={{0,2},{2,4},{4,6},{6,8},{8,10},{10,12},{12,14},{14,16},{16,18},{18... | collective-permute-start | bytes 73736 | tf_op jit(solution)/shard_map/ppermute | solution.py:17
  169.4 0.7 copy-start.8
  169.4 97.2 %copy-start.4 = (bf16[512,2048]{1,0:T(8,128)(2,1)S(1)}, bf16[512,2048]{1,0:T(8,128)(2,1)}, u32[]{:S(2)}) copy-start(bf16[512,2048]{1,0:T(8,128)(2,1)} %param.10) | copy-start | bytes 6291460
  169.4 166.0 %all-gather.6.cloned.1.call-start = ((), (), s32[]{:S(2)}) async-start(), calls=%async_computation.3 | async-start | bytes 6291456 | tf_op jit(solution)/shard_map/all_gather | solution.py:66
  277.4 317.1 %all-gather.8.cloned.1.call-start = ((), (), s32[]{:S(2)}) async-start(), calls=%async_computation.4 | async-start | bytes 53477376 | tf_op jit(solution)/shard_map/all_gather | solution.py:67
  632.8 30.2 %copy-start.1 = (bf16[512,1,2048]{2,0,1:T(8,128)(2,1)}, bf16[512,1,2048]{2,0,1:T(8,128)(2,1)S(1)}, u32[]{:S(2)}) copy-start(bf16[512,1,2048]{2,0,1:T(8,128)(2,1)S(1)} %fusion.3) | copy-start | bytes 6291460
  633.2 48.0 %collective-permute-start.1 = (bf16[128,128,16]{0,2,1:T(8,128)(2,1)S(1)}, bf16[128,128,16]{0,2,1:T(8,128)(2,1)S(1)}, u32[]{:S(2)}, u32[]{:S(2)}) collective-permute-start(bf16[128,128,16]{0,2,1:T(8,128)(2,1)S(1)} %bitcast.78), channel_id=1, source_target_pairs={{0,2},{2,4},{4,6},{6,8},{8,10},{10,12},{12,14},{14,16},{16,18},{18... | collective-permute-start | bytes 1572872 | tf_op jit(solution)/shard_map/ppermute | solution.py:17
  653.7 6.8 copy-start.6
  663.0 4.1 slice-start
  668.7 7.2 %copy-start.3 = (bf16[4,128,128,16]{1,0,3,2:T(4,128)(2,1)S(1)}, bf16[4,128,128,16]{1,0,3,2:T(4,128)(2,1)}, u32[]{:S(2)}) copy-start(bf16[4,128,128,16]{1,0,3,2:T(4,128)(2,1)} %convert_element_type.84) | copy-start | bytes 6291460
  675.9 5.3 copy-start.2
Sparse Core Ops, SparseCore 0:
  9.5 132.8 all-gather.3
  169.5 96.9 reduce-scatter.1
  277.5 57.8 all-gather.5
  336.8 257.5 all-gather.7
where the time goes:
time: 711 us; the launch traced here: 710 us
  waiting for transfers between devices  531 us (75%)
  matrix products  80 us (11%)
  local copies, waits for them, and re-layouts  44.8 us (6%)
  other arithmetic  28.9 us (4%)
  between operations  13.3 us (2%)
  starting transfers between devices  8.31 us (1%)
    all_gather x1, waiting for transfers between devices, per_device(): piece = lax.all_gather(w_in, 'seq', axis=0, tiled=True)  259 us
    all_gather x1, waiting for transfers between devices, project_out(): lax.all_gather(w_out, 'seq', axis=1, tiled=True)  121 us
    reduce_scatter x1, waiting for transfers between devices, per_device(): share = lax.psum_scatter(partial_out, 'tp', scatter_dimension=1, tiled=True)  96.5 us
    all_gather x1, waiting for transfers between devices, per_device(): gathered = lax.all_gather(normed, 'tp', axis=1, tiled=True)  53 us
    dot_general x1, matrix products, per_device(): jnp.dot(gathered, flat_piece, preferred_element_type=jnp.float32)  34.3 us
    dot_general x1, matrix products, project_out(): jnp.dot(y_se, lax.all_gather(w_out, 'seq', axis=1, tiled=True), preferred...  27 us
  transfers between devices with their start and end apart: 6, of which 4 were waited for; matrix products, arithmetic and copies ran while one was open for 8% of the time, Pallas kernels for 0%

commit v1 on v0

v1 whole, which is shorter than its diff:
```python
import functools
import jax
import jax.numpy as jnp
from jax import lax
from jax.experimental import pallas as pl
from jax.experimental.pallas import tpu as pltpu
from jax.sharding import PartitionSpec as P

GROUP = 16
SE_TAPS = 7
MR_TAPS = 128


norm_eps = 1e-05


def shifted(block, axis, distance):
    devices = range(lax.axis_size(axis))
    route = [(i - distance, i) for i in devices if i - distance in devices]
    return lax.ppermute(block, axis, route)


LANES = 128
PER_TILE = LANES // GROUP


def table_kernel(taps_ref, out_ref):
    lag = lax.broadcasted_iota(jnp.int32, (MR_TAPS, MR_TAPS), 0) - lax.broadcasted_iota(
        jnp.int32, (MR_TAPS, MR_TAPS), 1
    )
    for g in range(PER_TILE):
        row = jnp.broadcast_to(taps_ref[g : g + 1, :], (MR_TAPS, MR_TAPS))
        table = pltpu.roll(row, 0, 1, stride=1, stride_axis=0)
        rows = pl.ds(g * MR_TAPS, MR_TAPS)
        out_ref[rows, :MR_TAPS] = jnp.where(lag >= 0, table, 0.0).astype(jnp.bfloat16)
        out_ref[rows, MR_TAPS:] = jnp.where(lag < 0, table, 0.0).astype(jnp.bfloat16)


def filter_tables(taps):
    groups = taps.shape[0]
    wide = taps.astype(jnp.float32)
    flipped = jnp.concatenate([wide[:, :1], wide[:, :0:-1]], axis=1)
    return pl.pallas_call(
        table_kernel,
        grid=(groups // PER_TILE,),
        in_specs=[pl.BlockSpec((PER_TILE, MR_TAPS), lambda i: (i, 0))],
        out_specs=pl.BlockSpec((PER_TILE * MR_TAPS, 2 * MR_TAPS), lambda i: (i, 0)),
        out_shape=jax.ShapeDtypeStruct((groups * MR_TAPS, 2 * MR_TAPS), jnp.bfloat16),
        cost_estimate=pl.CostEstimate(
            flops=groups * MR_TAPS * MR_TAPS * 16, bytes_accessed=groups * MR_TAPS * MR_TAPS * 4, transcendentals=0
        ),
    )(flipped)


def conv_kernel(blocks, table_ref, u_ref, tail_ref, query_ref, skip_ref, out_ref):
    u = u_ref[...]
    now = jnp.concatenate([u[b * MR_TAPS : (b + 1) * MR_TAPS] for b in range(blocks)], axis=1)
    before = jnp.concatenate([tail_ref[...], now[:, : (blocks - 1) * LANES]], axis=1)
    rhs = jnp.concatenate([now, before], axis=0)
    owner = lax.rem(lax.broadcasted_iota(jnp.int32, (MR_TAPS, blocks * LANES), 1), LANES) // GROUP
    total = None
    for g in range(PER_TILE):
        part = jnp.dot(
            table_ref[g * MR_TAPS : (g + 1) * MR_TAPS, :], rhs, preferred_element_type=jnp.float32
        )
        total = part if total is None else jnp.where(owner == g, part, total)
    for b in range(blocks):
        rows = slice(b * MR_TAPS, (b + 1) * MR_TAPS)
        direct = skip_ref[...].astype(jnp.float32) * u[rows].astype(jnp.float32)
        conv = total[:, b * LANES : (b + 1) * LANES]
        out_ref[rows, :] = (query_ref[rows, :] * (conv + direct)).astype(jnp.bfloat16)


def long_conv(tables, u_mr, tail, query, skip):
    rows, width = u_mr.shape
    tile = lambda i: (0, i)
    return pl.pallas_call(
        functools.partial(conv_kernel, rows // MR_TAPS),
        grid=(width // LANES,),
        in_specs=[
            pl.BlockSpec((PER_TILE * MR_TAPS, 2 * MR_TAPS), lambda i: (i, 0)),
            pl.BlockSpec((rows, LANES), tile),
            pl.BlockSpec((MR_TAPS, LANES), tile),
            pl.BlockSpec((rows, LANES), tile),
            pl.BlockSpec((1, LANES), tile),
        ],
        out_specs=pl.BlockSpec((rows, LANES), tile),
        out_shape=jax.ShapeDtypeStruct((rows, width), jnp.bfloat16),
        compiler_params=pltpu.CompilerParams(vmem_limit_bytes=32 * 1024 * 1024),
        cost_estimate=pl.CostEstimate(
            flops=rows * width * 4096, bytes_accessed=rows * width * 16, transcendentals=0
        ),
    )(tables, u_mr, tail, query, skip.reshape(1, width))


def swap(block):
    return lax.ppermute(block, "tp", [(0, 1), (1, 0)])


def sum_over_tp(partial):
    if lax.axis_size("tp") != 2:
        return lax.psum_scatter(partial, "tp", scatter_dimension=1, tiled=True)
    half = partial.shape[1] // 2
    first = lax.axis_index("tp") == 0
    low, high = partial[:, :half], partial[:, half:]
    sent = jnp.where(first, high, low).astype(jnp.bfloat16)
    return jnp.where(first, low, high) + swap(sent).astype(jnp.float32)


def gather_tp(block):
    if lax.axis_size("tp") != 2:
        return lax.all_gather(block, "tp", axis=1, tiled=True)
    first = lax.axis_index("tp") == 0
    other = swap(block)
    return jnp.concatenate(
        [jnp.where(first, block, other), jnp.where(first, other, block)], axis=1
    )


def project_out(y_se, w_out):
    return jnp.dot(
        y_se, lax.all_gather(w_out, "seq", axis=1, tiled=True), preferred_element_type=jnp.float32
    )


def per_device(qkv_se, residual, taps_se, skip_se, w_out, norm_gain, w_in, taps_mr, skip_mr):
    row_count = qkv_se.shape[0]
    chan_width = qkv_se.shape[2]
    query_se = qkv_se[:, 0].astype(jnp.float32)
    u_se = (qkv_se[:, 1].astype(jnp.float32) * qkv_se[:, 2].astype(jnp.float32)).astype(
        jnp.bfloat16
    )
    incoming_se = shifted(u_se[row_count - (SE_TAPS - 1) :], "seq", 1)
    extended = jnp.concatenate([incoming_se, u_se], axis=0).astype(jnp.float32)
    per_channel = jnp.repeat(taps_se.astype(jnp.float32), GROUP, axis=0)
    conv_se = jnp.zeros((row_count, chan_width), jnp.float32)
    for tap_index in range(SE_TAPS):
        begin = SE_TAPS - 1 - tap_index
        conv_se = conv_se + per_channel[:, tap_index] * extended[begin : begin + row_count]
    y_se = (query_se * (conv_se + skip_se.astype(jnp.float32) * u_se.astype(jnp.float32))).astype(
        jnp.bfloat16
    )
    gain_full = norm_gain.astype(jnp.float32)
    partial_out = project_out(y_se, w_out)
    share = sum_over_tp(partial_out)
    stream = residual.astype(jnp.float32) + share
    squares = lax.psum(jnp.sum(stream * stream, axis=1), "tp")
    scale = lax.rsqrt(squares / (chan_width * lax.axis_size("tp")) + norm_eps)
    my_gain = lax.dynamic_slice_in_dim(gain_full, lax.axis_index("tp") * chan_width, chan_width, 0)
    normed = (stream * scale[:, None] * my_gain).astype(jnp.bfloat16)
    gathered = gather_tp(normed)
    piece = lax.all_gather(w_in, "seq", axis=0, tiled=True)
    flat_piece = piece.reshape(piece.shape[0], 3 * chan_width)
    proj = jnp.dot(gathered, flat_piece, preferred_element_type=jnp.float32).reshape(
        row_count, 3, chan_width
    )
    query_mr = proj[:, 0]
    u_mr = (proj[:, 1] * proj[:, 2]).astype(jnp.bfloat16)
    tail = shifted(u_mr[row_count - MR_TAPS :], "seq", 1)
    return long_conv(filter_tables(taps_mr), u_mr, tail, query_mr, skip_mr)


def solution(mesh):
    placed = (
        P("seq", None, "tp"),
        P("seq", "tp"),
        P("tp", None),
        P("tp"),
        P("tp", "seq"),
        P(),
        P("seq", None, "tp"),
        P("tp", None),
        P("tp"),
    )
    return jax.shard_map(
        per_device, mesh=mesh, in_specs=placed, out_specs=P("seq", "tp"), check_vma=False
    )
```

time: 711 us -> 477 us (0.67)
  waiting for transfers between devices: 531 us -> 321 us
  local copies, waits for them, and re-layouts: 44.8 us -> 12.3 us
  matrix products: 80 us -> 59.5 us
  Pallas kernels: 0 us -> 20 us
    all_gather x1, waiting for transfers between devices: 259 us -> 115 us  [per_device(): piece = lax.all_gather(w_in, 'seq', axis=0, tiled=True)]
    reduce_scatter x1 -> x0, waiting for transfers between devices: 96.5 us -> none  [per_device(): share = lax.psum_scatter(partial_out, 'tp', scatter_dimension=1, tiled=True)]
    ppermute x0 -> x2, waiting for transfers between devices: none -> 90.1 us  [swap(): return lax.ppermute(block, 'tp', [(0, 1), (1, 0)])]
    all_gather x1 -> x0, waiting for transfers between devices: 53 us -> none  [per_device(): gathered = lax.all_gather(normed, 'tp', axis=1, tiled=True)]
    pallas_call x0 -> x2, Pallas kernels: none -> 20 us  [the longest x1 10.1 us: long_conv(): pl.pallas_call(functools.partial(conv_kernel, rows // MR_TAPS), grid=(wid...]
    dot_general x3 -> x0, matrix products: 18.7 us -> none  [the longest x1 10.4 us: toeplitz_pair(): jnp.einsum('gj,jts->gts', taps, picks, preferred_element_type=jnp.float32)]
    select_n x2 -> x0, local copies, waits for them, and re-layouts: 13.4 us -> none  [the longest x1 6.75 us: toeplitz_pair(): upper = jnp.where(offsets[None] < 0, table, jnp.zeros_like(table))]
    convert_element_type x3 -> x1, other arithmetic: 13.2 us -> 3.84 us  [sum_over_tp(): sent = jnp.where(first, high, low).astype(jnp.bfloat16)]
  transfers between devices with their start and end apart: 6 -> 6, of which waited for: 4 -> 4; matrix products, arithmetic and copies ran while one was open for 8% -> 13% of each run, Pallas kernels for 0% -> 2%
where the time goes in v1:
time: 477 us
  waiting for transfers between devices  321 us (67%)
  matrix products  59.5 us (12%)
  other arithmetic  35.6 us (7%)
  Pallas kernels  20 us (4%)
  between operations  13.6 us (3%)
  local copies, waits for them, and re-layouts  12.3 us (3%)
  starting transfers between devices  10.3 us (2%)
    all_gather x1, waiting for transfers between devices, project_out(): lax.all_gather(w_out, 'seq', axis=1, tiled=True)  116 us
    all_gather x1, waiting for transfers between devices, per_device(): piece = lax.all_gather(w_in, 'seq', axis=0, tiled=True)  115 us
    ppermute x2, waiting for transfers between devices, swap(): return lax.ppermute(block, 'tp', [(0, 1), (1, 0)])  90.1 us
    dot_general x1, matrix products, per_device(): jnp.dot(gathered, flat_piece, preferred_element_type=jnp.float32)  32.5 us
    dot_general x1, matrix products, project_out(): jnp.dot(y_se, lax.all_gather(w_out, 'seq', axis=1, tiled=True), preferred...  27 us
    unnamed x19, local copies, waits for them, and re-layouts  11.6 us
    pallas_call x1, Pallas kernels, long_conv(): pl.pallas_call(functools.partial(conv_kernel, rows // MR_TAPS), grid=(wid...  10.1 us
    pallas_call x1, Pallas kernels, filter_tables(): pl.pallas_call(table_kernel, grid=(groups // PER_TILE,), in_specs=[pl.Blo...  9.97 us
  transfers between devices with their start and end apart: 6, of which 4 were waited for; matrix products, arithmetic and copies ran while one was open for 13% of the time, Pallas kernels for 2%

profile of v1, /device:TPU:1, one launch (start us, length us, event | category | flops | bytes accessed | tf_op | source)
XLA Modules:
  0.0 476.7 jit_solution(17898537732348145861)
XLA Ops:
  7.3 4.7 copy.12
  12.0 3.0 multiply_convert_fusion.1
  15.0 1.3 copy-done.3
  16.3 4.5 collective-permute-start
  21.3 3.2 fusion.30
  24.6 2.6 maximum_convert_fusion
  27.3 115.5 %all-gather.3.cloned.1.call-done = bf16[2048,4096]{1,0:T(8,128)(2,1)} async-done(((bf16[2048,256]{1,0:T(8,128)(2,1)}), bf16[2048,4096]{1,0:T(8,128)(2,1)}) %all-gather.3.cloned.1.call-update) | async-done | bytes 16777232 | tf_op jit(solution)/shard_map/all_gather | solution.py:122
  142.8 27.0 %fusion.14 = f32[512,4096]{1,0:T(8,128)} fusion(bf16[2048,4096]{1,0:T(8,128)(2,1)} %all-gather.3.cloned.1.call-done, f32[518,2048]{1,0:T(8,128)} %maximum_convert_fusion, f32[2048]{0:T(1024)S(1)} %convert_element_type.68, f32[2048]{0:T(1024)S(1)} %bitcast.41, f32[2048]{0:T(1024)S(1)} %bitcast.42, f32[2048]{0:T(1024)S(1)} %bitcast.43, ...), kind=kOutput, calls=%fused_computation.30 | convolution fusion | flops 8609857536 | bytes 58785792 | tf_op jit(solution)/shard_map/dot_general | solution.py:121
  169.7 3.8 select_convert_fusion
  174.8 45.9 %collective-permute-done.1 = bf16[512,2048]{1,0:T(8,128)(2,1)} collective-permute-done((bf16[512,2048]{1,0:T(8,128)(2,1)S(1)}, bf16[512,2048]{1,0:T(8,128)(2,1)}, u32[]{:S(2)}, u32[]{:S(2)}) %collective-permute-start.1) | collective-permute-done | bytes 2097184 | tf_op jit(solution)/shard_map/ppermute | solution.py:97
  220.7 8.9 %multiply_reduce_fusion = (f32[512]{0:T(512)S(1)}, f32[512,2048]{1,0:T(8,128)}) fusion(bf16[512,2048]{1,0:T(8,128)(2,1)} %collective-permute-done.1, f32[512,4096]{1,0:T(8,128)} %fusion.14, pred[]{:T(512)S(6)} %eq.4, bf16[512,2048]{1,0:T(8,128)(2,1)} %param.10), kind=kLoop, calls=%fused_computation.25 | loop fusion | flops 7339520 | bytes 16779264 | tf_op jit(solution)/shard_map/reduce_sum | solution.py:147
  229.7 4.3 psum.7
  234.0 2.8 multiply_convert_fusion
  236.9 1.3 collective-permute-start.2
  238.1 44.2 %collective-permute-done.2 = bf16[512,2048]{1,0:T(8,128)(2,1)S(1)} collective-permute-done((bf16[512,2048]{1,0:T(8,128)(2,1)S(1)}, bf16[512,2048]{1,0:T(8,128)(2,1)S(1)}, u32[]{:S(2)}, u32[]{:S(2)}) %collective-permute-start.2) | collective-permute-done | bytes 2097184 | tf_op jit(solution)/shard_map/ppermute | solution.py:97
  282.3 2.6 broadcast_select_fusion.1
  285.0 114.7 %all-gather.5.cloned.1.call-done = bf16[4096,3,2048]{0,2,1:T(8,128)(2,1)} async-done(((bf16[256,3,2048]{0,2,1:T(8,128)(2,1)}), bf16[4096,3,2048]{0,2,1:T(8,128)(2,1)}) %all-gather.5.cloned.1.call-update) | async-done | bytes 50331664 | tf_op jit(solution)/shard_map/all_gather | solution.py:152
  399.6 32.5 %fusion = f32[512,3,2048]{2,0,1:T(8,128)} fusion(bf16[4096,3,2048]{0,2,1:T(8,128)(2,1)} %all-gather.5.cloned.1.call-done, bf16[512,2048]{1,0:T(8,128)(2,1)} %get-tuple-element.10, bf16[512,2048]{1,0:T(8,128)(2,1)S(1)} %get-tuple-element.9), kind=kOutput, calls=%fused_computation | convolution fusion | flops 25778192384 | bytes 67108864 | tf_op jit(solution)/shard_map/dot_general | solution.py:154
  432.2 7.9 %slice_bitcast_fusion = (f32[512,2048]{1,0:T(8,128)}, bf16[512,1,2048]{2,0,1:T(8,128)(2,1)S(1)}) fusion(f32[512,3,2048]{2,0,1:T(8,128)} %fusion), kind=kLoop, calls=%fused_computation.2 | loop fusion | flops 2097152 | bytes 18874368 | tf_op jit(solution)/shard_map/squeeze | solution.py:157
  440.1 3.2 collective-permute-start.3
  444.2 10.0 %shard_map.91.table_ref = bf16[16384,256]{1,0:T(8,128)(2,1)} custom-call(f32[128,128]{1,0:T(8,128)} %pad_maximum_fusion.taps_ref), custom_call_target="tpu_custom_call" | custom-call | flops 33554432 | bytes 8388608 | tf_op jit(solution)/shard_map/pallas_call | solution.py:43
  454.2 3.4 copy-done
  457.6 2.2 copy-done.1
  459.8 10.1 %shard_map.92 = bf16[512,2048]{1,0:T(8,128)(2,1)} custom-call(bf16[16384,256]{1,0:T(8,128)(2,1)S(1)} %copy-done, bf16[512,2048]{1,0:T(8,128)(2,1)S(1)} %bitcast.39, bf16[128,2048]{1,0:T(8,128)(2,1)S(1)} %collective-permute-done.3.tail_ref, f32[512,2048]{1,0:T(8,128)S(1)} %copy-done.1, bf16[1,2048]{1,0:T(2,128)(2,1)S(1)} %reshape.33.skip_ref), custom_call_target="tpu_custom_call" | custom-call | flops 4294967296 | bytes 16777216 | tf_op jit(solution)/shard_map/pallas_call | solution.py:77
  (35 shorter events, 3.4 us)
Async XLA Ops:
  6.5 136.2 %all-gather.3.cloned.1.call-start = ((), (), s32[]{:S(2)}) async-start(), calls=%async_computation | async-start | bytes 17825792 | tf_op jit(solution)/shard_map/all_gather | solution.py:122
  7.3 392.4 %all-gather.5.cloned.1.call-start = ((), (), s32[]{:S(2)}) async-start(), calls=%async_computation.1 | async-start | bytes 53477376 | tf_op jit(solution)/shard_map/all_gather | solution.py:152
  12.0 8.9 %copy-start.7 = (bf16[128,7]{0,1:T(8,128)(2,1)S(1)}, bf16[128,7]{0,1:T(8,128)(2,1)}, u32[]{:S(2)}) copy-start(bf16[128,7]{0,1:T(8,128)(2,1)} %param.11) | copy-start | bytes 5380
  15.0 1.3 copy-start.3
  16.3 8.3 %copy-start.5 = (bf16[2048]{0:T(1024)(128)(2,1)S(1)}, bf16[2048]{0:T(1024)(128)(2,1)}, u32[]{:S(2)}) copy-start(bf16[2048]{0:T(1024)(128)(2,1)} %param.12) | copy-start | bytes 12292
  16.3 8.3 %collective-permute-start = (bf16[6,2048]{1,0:T(8,128)(2,1)S(1)}, bf16[6,2048]{1,0:T(8,128)(2,1)S(1)}, u32[]{:S(2)}, u32[]{:S(2)}) collective-permute-start(bf16[6,2048]{1,0:T(8,128)(2,1)S(1)} %slice_bitcast_fusion.2), channel_id=1, source_target_pairs={{0,2},{2,4},{4,6},{6,8},{8,10},{10,12},{12,14},{14,16},{16,18},{18... | collective-permute-start | bytes 73736 | tf_op jit(solution)/shard_map/ppermute | solution.py:20
  169.7 5.1 %copy-start.8 = (bf16[4096]{0:T(1024)(128)(2,1)S(1)}, bf16[4096]{0:T(1024)(128)(2,1)}, u32[]{:S(2)}) copy-start(bf16[4096]{0:T(1024)(128)(2,1)} %param.14) | copy-start | bytes 24580
  173.6 47.2 %collective-permute-start.1 = (bf16[512,2048]{1,0:T(8,128)(2,1)S(1)}, bf16[512,2048]{1,0:T(8,128)(2,1)}, u32[]{:S(2)}, u32[]{:S(2)}) collective-permute-start(bf16[512,2048]{1,0:T(8,128)(2,1)S(1)} %select_convert_fusion), channel_id=1, source_target_pairs={{0,1},{1,0},{2,3},{3,2},{4,5},{5,4},{6,7},{7,6},{8,9},{9,8},{10,11... | collective-permute-start | bytes 6291464 | tf_op jit(solution)/shard_map/ppermute | solution.py:97
  234.0 48.3 %copy-start.2 = (f32[512,2048]{1,0:T(8,128)S(1)}, f32[512,2048]{1,0:T(8,128)}, u32[]{:S(2)}) copy-start(f32[512,2048]{1,0:T(8,128)} %get-tuple-element.6) | copy-start | bytes 12582916
  236.9 45.5 %collective-permute-start.2 = (bf16[512,2048]{1,0:T(8,128)(2,1)S(1)}, bf16[512,2048]{1,0:T(8,128)(2,1)S(1)}, u32[]{:S(2)}, u32[]{:S(2)}) collective-permute-start(bf16[512,2048]{1,0:T(8,128)(2,1)S(1)} %multiply_convert_fusion), channel_id=1, source_target_pairs={{0,1},{1,0},{2,3},{3,2},{4,5},{5,4},{6,7},{7,6},{8,9},{9,8},{10,11... | collective-permute-start | bytes 6291464 | tf_op jit(solution)/shard_map/ppermute | solution.py:97
  432.2 11.2 %copy-start.4 = (bf16[128,128]{1,0:T(8,128)(2,1)S(1)}, bf16[128,128]{1,0:T(8,128)(2,1)}, u32[]{:S(2)}) copy-start(bf16[128,128]{1,0:T(8,128)(2,1)} %param.16) | copy-start | bytes 98308
  432.2 11.3 %copy-start.6 = (bf16[2048]{0:T(1024)(128)(2,1)S(1)}, bf16[2048]{0:T(1024)(128)(2,1)}, u32[]{:S(2)}) copy-start(bf16[2048]{0:T(1024)(128)(2,1)} %param.17) | copy-start | bytes 12292
  440.1 14.1 %collective-permute-start.3 = (bf16[128,2048]{1,0:T(8,128)(2,1)S(1)}, bf16[128,2048]{1,0:T(8,128)(2,1)S(1)}, u32[]{:S(2)}, u32[]{:S(2)}) collective-permute-start(bf16[128,2048]{1,0:T(8,128)(2,1)S(1)} %slice_bitcast_fusion.1), channel_id=1, source_target_pairs={{0,2},{2,4},{4,6},{6,8},{8,10},{10,12},{12,14},{14,16},{16,18},{18... | collective-permute-start | bytes 1572872 | tf_op jit(solution)/shard_map/ppermute | solution.py:20
  454.2 3.4 copy-start
  457.6 2.2 copy-start.1
Sparse Core Ops, SparseCore 0:
  9.5 133.2 all-gather.2
  144.3 255.2 all-gather.4

commit v2 on v1

--- a/solution.py
+++ b/solution.py
@@ -52,7 +52,7 @@
     )(flipped)
 
 
-def conv_kernel(blocks, table_ref, u_ref, tail_ref, query_ref, skip_ref, out_ref):
+def conv_kernel(blocks, table_ref, u_ref, tail_ref, skip_ref, out_ref):
     u = u_ref[...]
     now = jnp.concatenate([u[b * MR_TAPS : (b + 1) * MR_TAPS] for b in range(blocks)], axis=1)
     before = jnp.concatenate([tail_ref[...], now[:, : (blocks - 1) * LANES]], axis=1)
@@ -68,10 +68,10 @@
         rows = slice(b * MR_TAPS, (b + 1) * MR_TAPS)
         direct = skip_ref[...].astype(jnp.float32) * u[rows].astype(jnp.float32)
         conv = total[:, b * LANES : (b + 1) * LANES]
-        out_ref[rows, :] = (query_ref[rows, :] * (conv + direct)).astype(jnp.bfloat16)
-
-
-def long_conv(tables, u_mr, tail, query, skip):
+        out_ref[rows, :] = conv + direct
+
+
+def long_conv(tables, u_mr, tail, skip):
     rows, width = u_mr.shape
     tile = lambda i: (0, i)
     return pl.pallas_call(
@@ -81,16 +81,15 @@
             pl.BlockSpec((PER_TILE * MR_TAPS, 2 * MR_TAPS), lambda i: (i, 0)),
             pl.BlockSpec((rows, LANES), tile),
             pl.BlockSpec((MR_TAPS, LANES), tile),
-            pl.BlockSpec((rows, LANES), tile),
             pl.BlockSpec((1, LANES), tile),
         ],
         out_specs=pl.BlockSpec((rows, LANES), tile),
-        out_shape=jax.ShapeDtypeStruct((rows, width), jnp.bfloat16),
+        out_shape=jax.ShapeDtypeStruct((rows, width), jnp.float32),
         compiler_params=pltpu.CompilerParams(vmem_limit_bytes=32 * 1024 * 1024),
         cost_estimate=pl.CostEstimate(
             flops=rows * width * 4096, bytes_accessed=rows * width * 16, transcendentals=0
         ),
-    )(tables, u_mr, tail, query, skip.reshape(1, width))
+    )(tables, u_mr, tail, skip.reshape(1, width))
 
 
 def swap(block):
@@ -117,10 +116,29 @@
     )
 
 
-def project_out(y_se, w_out):
-    return jnp.dot(
-        y_se, lax.all_gather(w_out, "seq", axis=1, tiled=True), preferred_element_type=jnp.float32
-    )
+def out_kernel(y_ref, w_ref, out_ref):
+    out_ref[...] = jnp.dot(y_ref[...], w_ref[0], preferred_element_type=jnp.float32)
+
+
+def project_out(y_se, shards):
+    count, depth, width = shards.shape
+    rows = y_se.shape[0]
+    return pl.pallas_call(
+        out_kernel,
+        grid=(count,),
+        in_specs=[
+            pl.BlockSpec((rows, depth), lambda i: (0, 0)),
+            pl.BlockSpec((1, depth, width), lambda i: (i, 0, 0)),
+        ],
+        out_specs=pl.BlockSpec((rows, width), lambda i: (0, i)),
+        out_shape=jax.ShapeDtypeStruct((rows, count * width), jnp.float32),
+        compiler_params=pltpu.CompilerParams(vmem_limit_bytes=32 * 1024 * 1024),
+        cost_estimate=pl.CostEstimate(
+            flops=2 * rows * depth * count * width,
+            bytes_accessed=2 * count * depth * width + 4 * rows * count * width,
+            transcendentals=0,
+        ),
+    )(y_se, shards)
 
 
 def per_device(qkv_se, residual, taps_se, skip_se, w_out, norm_gain, w_in, taps_mr, skip_mr):
@@ -141,23 +159,30 @@
         jnp.bfloat16
     )
     gain_full = norm_gain.astype(jnp.float32)
-    partial_out = project_out(y_se, w_out)
+    out_full = lax.all_gather(w_out, "seq", axis=0, tiled=False)
+    w_query, w_key, w_value, out_full, y_se = lax.optimization_barrier(
+        (w_in[:, 0], w_in[:, 1], w_in[:, 2], out_full, y_se)
+    )
+    key_full = lax.all_gather(w_key, "seq", axis=0, tiled=True)
+    partial_out = project_out(y_se, out_full)
     share = sum_over_tp(partial_out)
+    w_value, key_full, share = lax.optimization_barrier((w_value, key_full, share))
+    value_full = lax.all_gather(w_value, "seq", axis=0, tiled=True)
     stream = residual.astype(jnp.float32) + share
     squares = lax.psum(jnp.sum(stream * stream, axis=1), "tp")
     scale = lax.rsqrt(squares / (chan_width * lax.axis_size("tp")) + norm_eps)
     my_gain = lax.dynamic_slice_in_dim(gain_full, lax.axis_index("tp") * chan_width, chan_width, 0)
     normed = (stream * scale[:, None] * my_gain).astype(jnp.bfloat16)
     gathered = gather_tp(normed)
-    piece = lax.all_gather(w_in, "seq", axis=0, tiled=True)
-    flat_piece = piece.reshape(piece.shape[0], 3 * chan_width)
-    proj = jnp.dot(gathered, flat_piece, preferred_element_type=jnp.float32).reshape(
-        row_count, 3, chan_width
-    )
-    query_mr = proj[:, 0]
-    u_mr = (proj[:, 1] * proj[:, 2]).astype(jnp.bfloat16)
+    key_mr = jnp.dot(gathered, key_full, preferred_element_type=jnp.float32)
+    w_query, value_full, key_mr = lax.optimization_barrier((w_query, value_full, key_mr))
+    query_full = lax.all_gather(w_query, "seq", axis=0, tiled=True)
+    value_mr = jnp.dot(gathered, value_full, preferred_element_type=jnp.float32)
+    u_mr = (key_mr * value_mr).astype(jnp.bfloat16)
     tail = shifted(u_mr[row_count - MR_TAPS :], "seq", 1)
-    return long_conv(filter_tables(taps_mr), u_mr, tail, query_mr, skip_mr)
+    gate = long_conv(filter_tables(taps_mr), u_mr, tail, skip_mr)
+    query_mr = jnp.dot(gathered, query_full, preferred_element_type=jnp.float32)
+    return (query_mr * gate).astype(jnp.bfloat16)
 
 
 def solution(mesh):

time: 477 us -> 549 us (1.15)
  waiting for transfers between devices: 321 us -> 406 us
  matrix products: 59.5 us -> 43.5 us
  Pallas kernels: 20 us -> 35.7 us
  other arithmetic: 35.6 us -> 22.9 us
    all_gather x2 -> x4, waiting for transfers between devices: 230 us -> 315 us  [the longest x1 110 us: per_device(): out_full = lax.all_gather(w_out, 'seq', axis=0, tiled=False)]
    pallas_call x0 -> x1, Pallas kernels: none -> 17.2 us  [project_out(): pl.pallas_call(out_kernel, grid=(count,), in_specs=[pl.BlockSpec((rows, d...]
    dot_general x2 -> x3, matrix products: 59.5 us -> 43.5 us  [the longest x1 15.2 us: per_device(): query_mr = jnp.dot(gathered, query_full, preferred_element_type=jnp.float32)]
    squeeze x1 -> x0, other arithmetic: 7.85 us -> none  [per_device(): query_mr = proj[:, 0]]
    reduce_sum x1, other arithmetic: 8.93 us -> 2.81 us  [per_device(): squares = lax.psum(jnp.sum(stream * stream, axis=1), 'tp')]
    unnamed x19 -> x26, local copies, waits for them, and re-layouts: 11.6 us -> 7.78 us
  transfers between devices with their start and end apart: 6 -> 8, of which waited for: 4 -> 6; matrix products, arithmetic and copies ran while one was open for 13% -> 10% of each run, Pallas kernels for 2% -> 7%
where the time goes in v2:
time: 549 us; the launch traced here: 548 us
  waiting for transfers between devices  406 us (74%)
  matrix products  43.5 us (8%)
  Pallas kernels  35.7 us (7%)
  other arithmetic  22.9 us (4%)
  between operations  13.4 us (2%)
  local copies, waits for them, and re-layouts  12 us (2%)
  starting transfers between devices  9.79 us (2%)
    all_gather x1, waiting for transfers between devices, per_device(): out_full = lax.all_gather(w_out, 'seq', axis=0, tiled=False)  110 us
    all_gather x1, waiting for transfers between devices, per_device(): query_full = lax.all_gather(w_query, 'seq', axis=0, tiled=True)  91.1 us
    ppermute x2, waiting for transfers between devices, swap(): return lax.ppermute(block, 'tp', [(0, 1), (1, 0)])  90.6 us
    all_gather x1, waiting for transfers between devices, per_device(): key_full = lax.all_gather(w_key, 'seq', axis=0, tiled=True)  58.9 us
    all_gather x1, waiting for transfers between devices, per_device(): value_full = lax.all_gather(w_value, 'seq', axis=0, tiled=True)  54.7 us
    pallas_call x1, Pallas kernels, project_out(): pl.pallas_call(out_kernel, grid=(count,), in_specs=[pl.BlockSpec((rows, d...  17.2 us
    dot_general x1, matrix products, per_device(): query_mr = jnp.dot(gathered, query_full, preferred_element_type=jnp.float32)  15.2 us
    dot_general x1, matrix products, per_device(): value_mr = jnp.dot(gathered, value_full, preferred_element_type=jnp.float32)  14.2 us
  transfers between devices with their start and end apart: 8, of which 6 were waited for; matrix products, arithmetic and copies ran while one was open for 10% of the time, Pallas kernels for 7%

profile of v2, /device:TPU:1, one launch (start us, length us, event | category | flops | bytes accessed | tf_op | source)
XLA Modules:
  0.0 547.8 jit_solution(4389631177221432592)
XLA Ops:
  7.3 3.0 multiply_convert_fusion.3
  10.4 4.8 collective-permute-start
  17.4 3.5 fusion.17
  21.0 1.8 slice_bitcast_fusion
  23.9 4.6 fusion.3.y_ref
  28.5 110.5 %all-gather.12.cloned.1.call-done = bf16[32768,256]{1,0:T(8,128)(2,1)} async-done(((bf16[2048,256]{1,0:T(8,128)(2,1)}), bf16[32768,256]{1,0:T(8,128)(2,1)}) %all-gather.12.cloned.1.call-update) | async-done | bytes 16777232 | tf_op jit(solution)/shard_map/all_gather | solution.py:162
  139.0 17.2 %shard_map.91 = f32[512,4096]{1,0:T(8,128)S(1)} custom-call(bf16[512,2048]{1,0:T(8,128)(2,1)S(1)} %fusion.3.y_ref, bf16[16,2048,256]{2,1,0:T(8,128)(2,1)} %bitcast.36), custom_call_target="tpu_custom_call" | custom-call | flops 8589934592 | bytes 25165824 | tf_op jit(solution)/shard_map/pallas_call | solution.py:126
  157.9 45.9 %collective-permute-done.1 = bf16[512,2048]{1,0:T(8,128)(2,1)S(1)} collective-permute-done((bf16[512,2048]{1,0:T(8,128)(2,1)S(1)}, bf16[512,2048]{1,0:T(8,128)(2,1)S(1)}, u32[]{:S(2)}, u32[]{:S(2)}) %collective-permute-start.1) | collective-permute-done | bytes 2097184 | tf_op jit(solution)/shard_map/ppermute | solution.py:96
  203.8 3.6 convert_add_fusion
  207.4 58.9 %all-gather.6.cloned.1.call-done = bf16[4096,2048]{1,0:T(8,128)(2,1)} async-done(((bf16[256,2048]{1,0:T(8,128)(2,1)}), bf16[4096,2048]{1,0:T(8,128)(2,1)}) %all-gather.6.cloned.1.call-update) | async-done | bytes 16777232 | tf_op jit(solution)/shard_map/all_gather | solution.py:166
  266.3 2.8 multiply_reduce_fusion
  269.1 4.0 psum.7
  273.1 3.3 multiply_convert_fusion.2
  277.7 44.8 %collective-permute-done.2 = bf16[512,2048]{1,0:T(8,128)(2,1)S(1)} collective-permute-done((bf16[512,2048]{1,0:T(8,128)(2,1)S(1)}, bf16[512,2048]{1,0:T(8,128)(2,1)S(1)}, u32[]{:S(2)}, u32[]{:S(2)}) %collective-permute-start.2) | collective-permute-done | bytes 2097184 | tf_op jit(solution)/shard_map/ppermute | solution.py:96
  324.8 14.1 %fusion.9 = f32[512,2048]{1,0:T(8,128)} fusion(bf16[4096,2048]{1,0:T(8,128)(2,1)} %all-gather.6.cloned.1.call-done, bf16[512,2048]{1,0:T(8,128)(2,1)S(1)} %get-tuple-element.28, bf16[512,2048]{1,0:T(8,128)(2,1)S(1)} %get-tuple-element.27), kind=kOutput, calls=%fused_computation.28 | convolution fusion | flops 8598323200 | bytes 25165824 | tf_op jit(solution)/shard_map/dot_general | solution.py:177
  338.8 54.7 %all-gather.8.cloned.1.call-done = bf16[4096,2048]{1,0:T(8,128)(2,1)} async-done(((bf16[256,2048]{1,0:T(8,128)(2,1)}), bf16[4096,2048]{1,0:T(8,128)(2,1)}) %all-gather.8.cloned.1.call-update) | async-done | bytes 16777232 | tf_op jit(solution)/shard_map/all_gather | solution.py:170
  393.5 14.2 %multiply_convert_fusion.1.u_ref = bf16[512,2048]{1,0:T(8,128)(2,1)S(1)} fusion(f32[512,2048]{1,0:T(8,128)} %fusion.9, bf16[4096,2048]{1,0:T(8,128)(2,1)} %all-gather.8.cloned.1.call-done, bf16[512,2048]{1,0:T(8,128)(2,1)} %copy-done.5, bf16[512,2048]{1,0:T(8,128)(2,1)} %copy-done.4), kind=kOutput, calls=%fused_computation.18 | convolution fusion | flops 8600420352 | bytes 27262976 | tf_op jit(solution)/shard_map/dot_general | solution.py:180
  407.8 2.3 collective-permute-start.3
  411.1 10.0 %shard_map.92.table_ref = bf16[16384,256]{1,0:T(8,128)(2,1)} custom-call(f32[128,128]{1,0:T(8,128)} %pad_maximum_fusion.4.taps_ref), custom_call_target="tpu_custom_call" | custom-call | flops 33554432 | bytes 8388608 | tf_op jit(solution)/shard_map/pallas_call | solution.py:43
  421.0 3.4 copy-done
  424.4 8.5 %shard_map.93 = f32[512,2048]{1,0:T(8,128)S(1)} custom-call(bf16[16384,256]{1,0:T(8,128)(2,1)S(1)} %copy-done, bf16[512,2048]{1,0:T(8,128)(2,1)S(1)} %multiply_convert_fusion.1.u_ref, bf16[128,2048]{1,0:T(8,128)(2,1)S(1)} %collective-permute-done.3.tail_ref, bf16[1,2048]{1,0:T(2,128)(2,1)S(1)} %reshape.24.skip_ref), custom_call_target="tpu_custom_call" | custom-call | flops 4294967296 | bytes 16777216 | tf_op jit(solution)/shard_map/pallas_call | solution.py:77
  433.0 1.9 copy-done.1
  434.9 91.1 %all-gather.10.cloned.1.call-done = bf16[4096,2048]{1,0:T(8,128)(2,1)} async-done(((bf16[256,2048]{1,0:T(8,128)(2,1)}), bf16[4096,2048]{1,0:T(8,128)(2,1)}) %all-gather.10.cloned.1.call-update) | async-done | bytes 16777232 | tf_op jit(solution)/shard_map/all_gather | solution.py:179
  526.0 15.2 %multiply_convert_fusion = bf16[512,2048]{1,0:T(8,128)(2,1)} fusion(f32[512,2048]{1,0:T(8,128)} %copy-done.1, bf16[4096,2048]{1,0:T(8,128)(2,1)} %all-gather.10.cloned.1.call-done, bf16[512,2048]{1,0:T(8,128)(2,1)} %copy-done.5, bf16[512,2048]{1,0:T(8,128)(2,1)} %copy-done.4), kind=kOutput, calls=%fused_computation.17 | convolution fusion | flops 8600420352 | bytes 27262976 | tf_op jit(solution)/shard_map/dot_general | solution.py:184
  (53 shorter events, 10.4 us)
Async XLA Ops:
  6.5 8.6 %copy-start.9 = (bf16[128,7]{0,1:T(8,128)(2,1)S(1)}, bf16[128,7]{0,1:T(8,128)(2,1)}, u32[]{:S(2)}) copy-start(bf16[128,7]{0,1:T(8,128)(2,1)} %param.11) | copy-start | bytes 5380
  6.5 132.4 %all-gather.12.cloned.1.call-start = ((), (), s32[]{:S(2)}) async-start(), calls=%async_computation.3 | async-start | bytes 17825792 | tf_op jit(solution)/shard_map/all_gather | solution.py:162
  7.3 259.0 %all-gather.6.cloned.1.call-start = ((), (), s32[]{:S(2)}) async-start(), calls=%async_computation | async-start | bytes 17825792 | tf_op jit(solution)/shard_map/all_gather | solution.py:166
  10.3 10.6 %copy-start.3 = (bf16[256,3,2048]{2,0,1:T(8,128)(2,1)S(1)}, bf16[256,3,2048]{2,0,1:T(8,128)(2,1)}, u32[]{:S(2)}) copy-start(bf16[256,3,2048]{2,0,1:T(8,128)(2,1)} %param.15) | copy-start | bytes 9437188
  10.4 12.5 %collective-permute-start = (bf16[6,2048]{1,0:T(8,128)(2,1)S(1)}, bf16[6,2048]{1,0:T(8,128)(2,1)S(1)}, u32[]{:S(2)}, u32[]{:S(2)}) collective-permute-start(bf16[6,2048]{1,0:T(8,128)(2,1)S(1)} %slice_bitcast_fusion.3), channel_id=1, source_target_pairs={{0,2},{2,4},{4,6},{6,8},{8,10},{10,12},{12,14},{14,16},{16,18},{18... | collective-permute-start | bytes 73736 | tf_op jit(solution)/shard_map/ppermute | solution.py:20
  17.4 6.1 %slice-start = ((s8[6291456]{0:T(1024)(128)(4,1)}), s8[4194304]{0:T(1024)(128)(4,1)S(1)}, s32[]{:S(2)}) async-start(s8[6291456]{0:T(1024)(128)(4,1)} %bitcast.27), calls=%async_computation.4 | async-start | bytes 8388608
  21.0 1.8 copy-start.7
  21.0 2.9 slice-start.1
  139.0 254.5 %all-gather.8.cloned.1.call-start = ((), (), s32[]{:S(2)}) async-start(), calls=%async_computation.1 | async-start | bytes 17825792 | tf_op jit(solution)/shard_map/all_gather | solution.py:170
  156.6 109.7 %copy-start.10 = (bf16[4096]{0:T(1024)(128)(2,1)S(1)}, bf16[4096]{0:T(1024)(128)(2,1)}, u32[]{:S(2)}) copy-start(bf16[4096]{0:T(1024)(128)(2,1)} %param.14) | copy-start | bytes 24580
  156.6 109.7 %copy-start.2 = (bf16[512,2048]{1,0:T(8,128)(2,1)S(1)}, bf16[512,2048]{1,0:T(8,128)(2,1)}, u32[]{:S(2)}) copy-start(bf16[512,2048]{1,0:T(8,128)(2,1)} %param.10) | copy-start | bytes 6291460
  156.6 47.2 %collective-permute-start.1 = (bf16[512,2048]{1,0:T(8,128)(2,1)S(1)}, bf16[512,2048]{1,0:T(8,128)(2,1)S(1)}, u32[]{:S(2)}, u32[]{:S(2)}) collective-permute-start(bf16[512,2048]{1,0:T(8,128)(2,1)S(1)} %select_convert_fusion), channel_id=1, source_target_pairs={{0,1},{1,0},{2,3},{3,2},{4,5},{5,4},{6,7},{7,6},{8,9},{9,8},{10,11... | collective-permute-start | bytes 6291464 | tf_op jit(solution)/shard_map/ppermute | solution.py:96
  266.2 259.8 %all-gather.10.cloned.1.call-start = ((), (), s32[]{:S(2)}) async-start(), calls=%async_computation.2 | async-start | bytes 17825792 | tf_op jit(solution)/shard_map/all_gather | solution.py:179
  276.5 46.0 %collective-permute-start.2 = (bf16[512,2048]{1,0:T(8,128)(2,1)S(1)}, bf16[512,2048]{1,0:T(8,128)(2,1)S(1)}, u32[]{:S(2)}, u32[]{:S(2)}) collective-permute-start(bf16[512,2048]{1,0:T(8,128)(2,1)S(1)} %multiply_convert_fusion.2), channel_id=1, source_target_pairs={{0,1},{1,0},{2,3},{3,2},{4,5},{5,4},{6,7},{7,6},{8,9},{9,8},{10,11... | collective-permute-start | bytes 6291464 | tf_op jit(solution)/shard_map/ppermute | solution.py:96
  322.8 1.4 copy-start.4
  322.8 2.0 copy-start.5
  393.5 16.6 %copy-start.6 = (bf16[128,128]{1,0:T(8,128)(2,1)S(1)}, bf16[128,128]{1,0:T(8,128)(2,1)}, u32[]{:S(2)}) copy-start(bf16[128,128]{1,0:T(8,128)(2,1)} %param.16) | copy-start | bytes 98308
  393.5 16.8 %copy-start.8 = (bf16[2048]{0:T(1024)(128)(2,1)S(1)}, bf16[2048]{0:T(1024)(128)(2,1)}, u32[]{:S(2)}) copy-start(bf16[2048]{0:T(1024)(128)(2,1)} %param.17) | copy-start | bytes 12292
  407.8 13.2 %collective-permute-start.3 = (bf16[128,2048]{1,0:T(8,128)(2,1)S(1)}, bf16[128,2048]{1,0:T(8,128)(2,1)S(1)}, u32[]{:S(2)}, u32[]{:S(2)}) collective-permute-start(bf16[128,2048]{1,0:T(8,128)(2,1)S(1)} %slice.127), channel_id=1, source_target_pairs={{0,2},{2,4},{4,6},{6,8},{8,10},{10,12},{12,14},{14,16},{16,18},{18... | collective-permute-start | bytes 1572872 | tf_op jit(solution)/shard_map/ppermute | solution.py:20
  421.0 3.4 copy-start
  433.0 1.9 copy-start.1
Sparse Core Ops, SparseCore 0:
  9.5 129.3 all-gather.11
  141.1 125.0 all-gather.5
  268.4 125.0 all-gather.7
  395.5 130.4 all-gather.9
